TPU v7x, 128 devices: a whole 4x4x4 slice. The times are simulated.
128 devices in a mesh: dp: 32 (over x, y, z_hi), narrow: 4 (over z_lo, core).
Axes of the slice: x: 4, y: 4, z: 4 (z_hi: 2, z_lo: 2; z = z_hi * 2 + z_lo), core: 2. Of those that a mesh axis runs over, the one named last changes fastest.
Arguments:
- picture_features: bfloat16 [98304, 1152], P(('dp', 'narrow')), may hold values from -1.0234375 to 1.0234375
- caption_features: bfloat16 [98304, 1152], P(('dp', 'narrow')), may hold values from -1.0234375 to 1.0234375
- match_identifiers: int32 [98304], replicated, may hold values from 0 to 767
- trading_step_number: int32 [1], replicated, may hold values from 1 to 31
- sharpness_coefficient: float32 [1], replicated, may hold values from 0.5 to 2
- offset_term: float32 [1], replicated, may hold values from -2 to 0
Outputs:
- grad_image: float32 [98304, 1152], P(('dp', 'narrow'))
- text_embedding_gradient: float32 [98304, 1152], P(('dp', 'narrow'))
- row_loss: float32 [98304], P(('dp', 'narrow'))
All inputs are finite; a program needn't handle non-finite values.
Results may differ from a plain program's by a relative error of at most 0.0034.
Values may be sent and summed in bfloat16 or wider, within the bound.
No kernel may reach another device: no remote copies, remote signals or barrier semaphores. Data moves between devices by JAX's collectives and lax.ppermute only.
A program may use at most 128 MiB of HBM per device.

v0:
```python
import jax
import jax.numpy as jnp
from jax import lax
from jax.experimental import pallas as pl
from jax.experimental.pallas import tpu as pltpu
from jax.sharding import PartitionSpec as P

AXES = ("dp", "narrow")
FINAL_ROWS = 192


def xor_route(count, mask):
    return [(d, d ^ mask) for d in range(count)]


def log1p(q):
    small = q * (1.0 - q * (0.5 - q * (1.0 / 3.0)))
    return jnp.where(q < 0.01, small, jnp.log(1.0 + q))


def pair_terms(logits, left_ids, right_ids):
    same = left_ids[:, None] == right_ids[None, :]
    z = jnp.where(same, logits, -logits)
    pair_loss = jnp.maximum(-z, 0.0) + log1p(jnp.exp(-jnp.abs(logits)))
    share = jnp.exp(-(pair_loss + z))
    coef = jnp.where(same, -share, share).astype(jnp.bfloat16)
    return pair_loss, coef


def dot(a, b, dims):
    return lax.dot_general(a, b, (dims, ((), ())), preferred_element_type=jnp.float32)


def final_call(image_parts, image_far_part, text_grad):
    rows, width = text_grad.shape

    def body(image_part, image_far_part, text_grad, image_out, text_out):
        image_out[...] = image_part[...] + image_far_part[...].astype(jnp.float32)
        text_out[...] = text_grad[...].astype(jnp.float32)

    block = pl.BlockSpec((FINAL_ROWS, width), lambda s: (s, 0))
    return pl.pallas_call(
        body,
        grid=(rows // FINAL_ROWS,),
        in_specs=[block] * 3,
        out_specs=[block] * 2,
        out_shape=[jax.ShapeDtypeStruct((rows, width), jnp.float32)] * 2,
        compiler_params=pltpu.CompilerParams(vmem_limit_bytes=20 * 2**20),
        cost_estimate=pl.CostEstimate(
            flops=rows * width, bytes_accessed=16 * rows * width, transcendentals=0
        ),
    )(image_parts, image_far_part, text_grad)


def partner_mask(rnd, width):
    return rnd * width ^ (rnd & 1) * (width // 2)


def solution(mesh):
    groups, width = mesh.shape["dp"], mesh.shape["narrow"]
    count, half = groups * width, width // 2
    over_z = xor_route(count, half)
    over_core = xor_route(count, 1)

    def over_dp(rnd, block):
        return lax.ppermute(block, AXES, xor_route(count, partner_mask(rnd, width)))

    def by_round(step, which, *args):
        branches = [lambda *a, r=r: step(r, *a) for r in range(1, groups)]
        return lax.switch(which, branches, *args)

    def per_device(picture, caption, ids, rnd, scale, shift):
        rnd, scale, shift = rnd[0], scale[0], shift[0]
        rows = picture.shape[0]
        me = lax.axis_index("dp") * width + lax.axis_index("narrow")
        text_at = me ^ partner_mask(rnd, width)
        take = lambda device: lax.dynamic_slice_in_dim(ids, device * rows, rows)
        image_ids = jnp.concatenate([take(me), take(me ^ half)])
        text_ids = jnp.concatenate([take(text_at), take(text_at ^ 1)])

        image_far = lax.ppermute(picture, AXES, over_z)
        text_own = by_round(over_dp, rnd - 1, caption)
        text_near = lax.ppermute(text_own, AXES, over_core)
        images = jnp.concatenate([picture, image_far])
        texts = jnp.concatenate([text_own, text_near])

        logits = scale * dot(images, texts, ((1,), (1,))) + shift
        pair_loss, coef = pair_terms(logits, image_ids, text_ids)
        loss_sum = jnp.sum(pair_loss, axis=1)

        text_parts = lax.optimization_barrier(scale * dot(coef, images, ((0,), (0,))))
        text_far_part = lax.ppermute(text_parts[rows:], AXES, over_core)
        image_parts = lax.optimization_barrier(scale * dot(coef, texts, ((1,), (0,))))
        image_far_part = image_parts[rows:].astype(jnp.bfloat16)
        text_part = (text_parts[:rows] + text_far_part).astype(jnp.bfloat16)

        loss_far = lax.ppermute(loss_sum[rows:], AXES, over_z)
        image_far_part, loss_far = lax.optimization_barrier((image_far_part, loss_far))
        image_far_part = lax.ppermute(image_far_part, AXES, over_z)
        text_grad = by_round(over_dp, rnd - 1, text_part)
        text_grad, image_far_part = lax.optimization_barrier((text_grad, image_far_part))
        image_grad, text_grad = final_call(image_parts, image_far_part, text_grad)
        row_loss = (loss_sum[:rows] + loss_far) / (rows * width)
        return image_grad, text_grad, row_loss

    in_specs = (P(AXES, None), P(AXES, None), P(), P(), P(), P())
    out_specs = (P(AXES, None), P(AXES, None), P(AXES))
    return jax.shard_map(
        per_device, mesh=mesh, in_specs=in_specs, out_specs=out_specs, check_vma=False
    )
```

profile of v0, /device:TPU:0, one launch (start us, length us, event | category | flops | bytes accessed | tf_op | source)
XLA Modules:
  0.0 151.6 jit_solution(16891410509097158827)
XLA Ops:
  0.6 2.1 %collective-permute-start.62 = (bf16[768,1152]{1,0:T(8,128)(2,1)}, bf16[768,1152]{1,0:T(8,128)(2,1)S(1)}, u32[]{:S(2)}, u32[]{:S(2)}) collective-permute-start(bf16[768,1152]{1,0:T(8,128)(2,1)} %param.68), channel_id=1, source_target_pairs={{0,2},{1,3},{2,0},{3,1},{4,6},{5,7},{6,4},{7,5},{8,10},{9,11},{10,... | collective-permute-start | bytes 5308424 | tf_op jit(solution)/shard_map/ppermute | solution.py:81
  3.4 45.0 %conditional.2 = (bf16[768,1152]{1,0:T(8,128)(2,1)}) conditional(s32[]{:T(128)} %bitcast.2, bf16[768,1152]{1,0:T(8,128)(2,1)} %param.69, bf16[768,1152]{1,0:T(8,128)(2,1)} %param.69, bf16[768,1152]{1,0:T(8,128)(2,1)} %param.69, bf16[768,1152]{1,0:T(8,128)(2,1)} %param.69, bf16[768,1152]{1,0:T(8,128)(2,1)} %param.69, ...), branch_computations={%region_0.0_spmd, %region_1.0_spmd, %region_2.0_spmd, %region_3.0_... | conditional | bytes 7077936 | solution.py:70
  3.4 6.2 %collective-permute-start.12 = (bf16[768,1152]{1,0:T(8,128)(2,1)}, bf16[768,1152]{1,0:T(8,128)(2,1)}, u32[]{:S(2)}, u32[]{:S(2)}) collective-permute-start(bf16[768,1152]{1,0:T(8,128)(2,1)} %param.12), channel_id=1, source_target_pairs={{0,54},{1,55},{2,52},{3,53},{4,50},{5,51},{6,48},{7,49},{8,62},{9,... | collective-permute-start | bytes 5308424 | tf_op jit(solution)/shard_map/cond/branch_12_fun/ppermute | solution.py:66
  9.6 38.8 %collective-permute-done.12 = bf16[768,1152]{1,0:T(8,128)(2,1)} collective-permute-done((bf16[768,1152]{1,0:T(8,128)(2,1)}, bf16[768,1152]{1,0:T(8,128)(2,1)}, u32[]{:S(2)}, u32[]{:S(2)}) %collective-permute-start.12) | collective-permute-done | bytes 1769504 | tf_op jit(solution)/shard_map/cond/branch_12_fun/ppermute | solution.py:66
  48.4 0.2 collective-permute-start.63
  49.9 0.9 fusion.7
  50.8 1.6 %constant_dynamic-update-slice_fusion.1 = bf16[1536,1152]{1,0:T(8,128)(2,1)S(1)} fusion(bf16[768,1152]{1,0:T(8,128)(2,1)} %param.68), kind=kLoop, calls=%fused_computation.17 | loop fusion | bytes 3538944
  52.4 0.0 collective-permute-done.62
  52.4 0.3 constant_dynamic-update-slice_fusion
  52.7 15.5 %fusion.3 = (f32[1536]{0:T(1024)S(1)}, bf16[1536,1536]{0,1:T(8,128)(2,1)S(1)}) fusion(s32[1536]{0:T(1024)S(1)} %get-tuple-element.148, s32[1536]{0:T(1024)S(1)} %get-tuple-element.147, f32[]{:T(128)} %bitcast.11, bf16[1536,1152]{1,0:T(8,128)(2,1)S(1)} %constant_dynamic-update-slice_fusion, bf16[768,1152]{1,0:T(8,128)(2,1)S(1)} %collective-permute-done.63, ...), kind=kOutput, calls=%fused_computation.13 | convolution fusion | flops 5499517440 | bytes 11814920 | tf_op jit(solution)/shard_map/dot_general | solution.py:31
  68.2 6.3 %convolution_multiply_fusion = f32[1536,1152]{1,0:T(8,128)S(1)} fusion(bf16[1536,1536]{0,1:T(8,128)(2,1)S(1)} %get-tuple-element.142, bf16[1536,1152]{1,0:T(8,128)(2,1)S(1)} %constant_dynamic-update-slice_fusion, f32[]{:T(128)} %bitcast.10), kind=kOutput, calls=%fused_computation.2 | convolution fusion | flops 5437587456 | bytes 15335428 | tf_op jit(solution)/shard_map/dot_general | solution.py:31
  74.6 0.2 slice.22
  74.8 0.6 collective-permute-start.64
  75.4 12.0 %collective-permute-start.65 = (f32[768]{0:T(1024)S(1)}, f32[768]{0:T(1024)S(1)}, u32[]{:S(2)}, u32[]{:S(2)}) collective-permute-start(f32[768]{0:T(1024)S(1)} %slice.24), channel_id=1, source_target_pairs={{0,2},{1,3},{2,0},{3,1},{4,6},{5,7},{6,4},{7,5},{8,10},{9,11},{10,... | collective-permute-start | bytes 9224 | tf_op jit(solution)/shard_map/ppermute | solution.py:97
  87.3 8.1 %convolution_multiply_fusion.1.image_part = f32[1536,1152]{1,0:T(8,128)S(1)} fusion(bf16[1536,1536]{0,1:T(8,128)(2,1)S(1)} %get-tuple-element.142, f32[]{:T(128)} %bitcast.8, bf16[768,1152]{1,0:T(8,128)(2,1)S(1)} %collective-permute-done.63, bf16[768,1152]{1,0:T(8,128)(2,1)} %get-tuple-element.149), kind=kOutput, calls=%fused_computation.3 | convolution fusion | flops 5444665344 | bytes 15335428 | tf_op jit(solution)/shard_map/dot_general | solution.py:31
  95.4 0.2 slice.33
  95.6 1.3 collective-permute-start.66
  96.9 1.2 fusion.4
  98.0 0.5 fusion.2
  98.5 45.0 %conditional.3 = (bf16[768,1152]{1,0:T(8,128)(2,1)}) conditional(s32[]{:T(128)} %bitcast.2, bf16[768,1152]{1,0:T(8,128)(2,1)S(1)} %fusion.2, bf16[768,1152]{1,0:T(8,128)(2,1)S(1)} %fusion.2, bf16[768,1152]{1,0:T(8,128)(2,1)S(1)} %fusion.2, bf16[768,1152]{1,0:T(8,128)(2,1)S(1)} %fusion.2, ...), branch_computations={%region_31.32_spmd, %region_32.33_spmd, %region_33.34_spmd, %regio... | conditional | bytes 7077936 | solution.py:70
  98.5 6.0 %collective-permute-start.43 = (bf16[768,1152]{1,0:T(8,128)(2,1)S(1)}, bf16[768,1152]{1,0:T(8,128)(2,1)}, u32[]{:S(2)}, u32[]{:S(2)}) collective-permute-start(bf16[768,1152]{1,0:T(8,128)(2,1)S(1)} %param.43), channel_id=1, source_target_pairs={{0,54},{1,55},{2,52},{3,53},{4,50},{5,51},{6,48},{7,49},{8,62},{9,... | collective-permute-start | bytes 5308424 | tf_op jit(solution)/shard_map/cond/branch_12_fun/ppermute | solution.py:66
  104.6 39.0 %collective-permute-done.43 = bf16[768,1152]{1,0:T(8,128)(2,1)} collective-permute-done((bf16[768,1152]{1,0:T(8,128)(2,1)S(1)}, bf16[768,1152]{1,0:T(8,128)(2,1)}, u32[]{:S(2)}, u32[]{:S(2)}) %collective-permute-start.43) | collective-permute-done | bytes 1769504 | tf_op jit(solution)/shard_map/cond/branch_12_fun/ppermute | solution.py:66
  143.6 3.0 %copy-done.1 = f32[1536,1152]{1,0:T(8,128)S(1)} copy-done((f32[1536,1152]{1,0:T(8,128)S(1)}, f32[1536,1152]{1,0:T(8,128)}, u32[]{:S(2)}) %copy-start.1) | copy-done | bytes 7077912
  146.6 4.8 %shard_map.178 = (f32[768,1152]{1,0:T(8,128)}, f32[768,1152]{1,0:T(8,128)}) custom-call(f32[1536,1152]{1,0:T(8,128)S(1)} %copy-done.1, bf16[768,1152]{1,0:T(8,128)(2,1)S(1)} %collective-permute-done.66.image_far_part, bf16[768,1152]{1,0:T(8,128)(2,1)} %get-tuple-element.150.text_grad), custom_call_target="tpu_custom_call" | custom-call | flops 884736 | bytes 14155776 | tf_op jit(solution)/shard_map/pallas_call | solution.py:42
  (9 shorter events, 0.0 us)
Async XLA Ops:
  0.6 51.8 %collective-permute-start.62 = (bf16[768,1152]{1,0:T(8,128)(2,1)}, bf16[768,1152]{1,0:T(8,128)(2,1)S(1)}, u32[]{:S(2)}, u32[]{:S(2)}) collective-permute-start(bf16[768,1152]{1,0:T(8,128)(2,1)} %param.68), channel_id=1, source_target_pairs={{0,2},{1,3},{2,0},{3,1},{4,6},{5,7},{6,4},{7,5},{8,10},{9,11},{10,... | collective-permute-start | bytes 5308424 | tf_op jit(solution)/shard_map/ppermute | solution.py:81
  3.4 45.0 %collective-permute-start.12 = (bf16[768,1152]{1,0:T(8,128)(2,1)}, bf16[768,1152]{1,0:T(8,128)(2,1)}, u32[]{:S(2)}, u32[]{:S(2)}) collective-permute-start(bf16[768,1152]{1,0:T(8,128)(2,1)} %param.12), channel_id=1, source_target_pairs={{0,54},{1,55},{2,52},{3,53},{4,50},{5,51},{6,48},{7,49},{8,62},{9,... | collective-permute-start | bytes 5308424 | tf_op jit(solution)/shard_map/cond/branch_12_fun/ppermute | solution.py:66
  48.4 4.4 %collective-permute-start.63 = (bf16[768,1152]{1,0:T(8,128)(2,1)}, bf16[768,1152]{1,0:T(8,128)(2,1)S(1)}, u32[]{:S(2)}, u32[]{:S(2)}) collective-permute-start(bf16[768,1152]{1,0:T(8,128)(2,1)} %get-tuple-element.149), channel_id=1, source_target_pairs={{0,1},{1,0},{2,3},{3,2},{4,5},{5,4},{6,7},{7,6},{8,9},{9,8},{10,11... | collective-permute-start | bytes 5308424 | tf_op jit(solution)/shard_map/ppermute | solution.py:83
  74.8 23.2 %collective-permute-start.64 = (f32[768,1152]{1,0:T(8,128)S(1)}, f32[768,1152]{1,0:T(8,128)S(1)}, u32[]{:S(2)}, u32[]{:S(2)}) collective-permute-start(f32[768,1152]{1,0:T(8,128)S(1)} %slice.22), channel_id=1, source_target_pairs={{0,1},{1,0},{2,3},{3,2},{4,5},{5,4},{6,7},{7,6},{8,9},{9,8},{10,11... | collective-permute-start | bytes 10616840 | tf_op jit(solution)/shard_map/ppermute | solution.py:92
  75.4 20.2 %collective-permute-start.65 = (f32[768]{0:T(1024)S(1)}, f32[768]{0:T(1024)S(1)}, u32[]{:S(2)}, u32[]{:S(2)}) collective-permute-start(f32[768]{0:T(1024)S(1)} %slice.24), channel_id=1, source_target_pairs={{0,2},{1,3},{2,0},{3,1},{4,6},{5,7},{6,4},{7,5},{8,10},{9,11},{10,... | collective-permute-start | bytes 9224 | tf_op jit(solution)/shard_map/ppermute | solution.py:97
  95.4 3.1 %copy-start = (f32[1536,1152]{1,0:T(8,128)}, f32[1536,1152]{1,0:T(8,128)S(1)}, u32[]{:S(2)}) copy-start(f32[1536,1152]{1,0:T(8,128)S(1)} %convolution_multiply_fusion.1.image_part) | copy-start | bytes 21233668
  95.6 47.9 %collective-permute-start.66 = (bf16[768,1152]{1,0:T(8,128)(2,1)S(1)}, bf16[768,1152]{1,0:T(8,128)(2,1)S(1)}, u32[]{:S(2)}, u32[]{:S(2)}) collective-permute-start(bf16[768,1152]{1,0:T(8,128)(2,1)S(1)} %slice.33), channel_id=1, source_target_pairs={{0,2},{1,3},{2,0},{3,1},{4,6},{5,7},{6,4},{7,5},{8,10},{9,11},{10,... | collective-permute-start | bytes 5308424 | tf_op jit(solution)/shard_map/ppermute | solution.py:99
  98.5 45.0 %collective-permute-start.43 = (bf16[768,1152]{1,0:T(8,128)(2,1)S(1)}, bf16[768,1152]{1,0:T(8,128)(2,1)}, u32[]{:S(2)}, u32[]{:S(2)}) collective-permute-start(bf16[768,1152]{1,0:T(8,128)(2,1)S(1)} %param.43), channel_id=1, source_target_pairs={{0,54},{1,55},{2,52},{3,53},{4,50},{5,51},{6,48},{7,49},{8,62},{9,... | collective-permute-start | bytes 5308424 | tf_op jit(solution)/shard_map/cond/branch_12_fun/ppermute | solution.py:66
  143.6 3.0 %copy-start.1 = (f32[1536,1152]{1,0:T(8,128)S(1)}, f32[1536,1152]{1,0:T(8,128)}, u32[]{:S(2)}) copy-start(f32[1536,1152]{1,0:T(8,128)} %copy-done) | copy-start | bytes 21233668
where the time goes:
time: 153 us; the launch traced here: 152 us
  waiting for transfers between devices  77.8 us (51%)
  matrix products  29.9 us (20%)
  starting transfers between devices  28.3 us (18%)
  local copies, waits for them, and re-layouts  6.18 us (4%)
  Pallas kernels  4.82 us (3%)
  between operations  2.9 us (2%)
  other arithmetic  1.62 us (1%)
    ppermute x2, waiting for transfers between devices, over_dp(): return lax.ppermute(block, AXES, xor_route(count, partner_mask(rnd, width)))  77.8 us
    dot_general x3, matrix products, dot(): lax.dot_general(a, b, (dims, ((), ())), preferred_element_type=jnp.float32)  29.9 us
    ppermute x2, starting transfers between devices, over_dp(): return lax.ppermute(block, AXES, xor_route(count, partner_mask(rnd, width)))  12.2 us
    ppermute x1, starting transfers between devices, per_device(): loss_far = lax.ppermute(loss_sum[rows:], AXES, over_z)  12 us
    pallas_call x1, Pallas kernels, final_call(): pl.pallas_call(body, grid=(rows // FINAL_ROWS,), in_specs=[block] * 3, ou...  4.82 us
    unnamed x5, local copies, waits for them, and re-layouts  4.63 us
  transfers between devices with their start and end apart: 7, of which 2 were waited for; matrix products, arithmetic and copies ran while one was open for 8% of the time, Pallas kernels for 0%

commit v1 on v0

--- a/solution.py
+++ b/solution.py
@@ -6,6 +6,10 @@
 from jax.sharding import PartitionSpec as P
 
 AXES = ("dp", "narrow")
+LOG1P = (
+    0.99999994, -0.499994934, 0.333190948, -0.248429745, 0.191059798,
+    -0.136631876, 0.0782252625, -0.0295048114, 0.00523258746,
+)
 FINAL_ROWS = 192
 
 
@@ -14,8 +18,10 @@
 
 
 def log1p(q):
-    small = q * (1.0 - q * (0.5 - q * (1.0 / 3.0)))
-    return jnp.where(q < 0.01, small, jnp.log(1.0 + q))
+    ratio = jnp.full_like(q, LOG1P[-1])
+    for factor in LOG1P[-2::-1]:
+        ratio = ratio * q + factor
+    return q * ratio
 
 
 def pair_terms(logits, left_ids, right_ids):
@@ -45,7 +51,7 @@
         in_specs=[block] * 3,
         out_specs=[block] * 2,
         out_shape=[jax.ShapeDtypeStruct((rows, width), jnp.float32)] * 2,
-        compiler_params=pltpu.CompilerParams(vmem_limit_bytes=20 * 2**20),
+        compiler_params=pltpu.CompilerParams(vmem_limit_bytes=58 * 2**20),
         cost_estimate=pl.CostEstimate(
             flops=rows * width, bytes_accessed=16 * rows * width, transcendentals=0
         ),

time: 153 us -> 134 us (0.88); the launches traced: 152 us -> 135 us
  starting transfers between devices: 28.3 us -> 9.94 us
  matrix products: 29.9 us -> 32.1 us
  local copies, waits for them, and re-layouts: 6.18 us -> 4.48 us
    ppermute x1, starting transfers between devices: 12 us -> 0.29 us  [per_device(): loss_far = lax.ppermute(loss_sum[rows:], AXES, over_z)]
    ppermute x2, starting transfers between devices: 12.2 us -> 5.17 us  [over_dp(): return lax.ppermute(block, AXES, xor_route(count, partner_mask(rnd, width)))]
    dot_general x3, matrix products: 29.9 us -> 32.1 us  [dot(): lax.dot_general(a, b, (dims, ((), ())), preferred_element_type=jnp.float32)]
    unnamed x5, local copies, waits for them, and re-layouts: 4.63 us -> 2.93 us
  transfers between devices with their start and end apart: 7 -> 7, of which waited for: 2 -> 2; matrix products, arithmetic and copies ran while one was open for 8% -> 9% of each run, Pallas kernels for 0% -> 0%
where the time goes in v1:
time: 134 us; the launch traced here: 135 us
  waiting for transfers between devices  77.9 us (58%)
  matrix products  32.1 us (24%)
  starting transfers between devices  9.94 us (7%)
  Pallas kernels  6.22 us (5%)
  local copies, waits for them, and re-layouts  4.48 us (3%)
  between operations  2.69 us (2%)
  other arithmetic  1.36 us (1%)
    ppermute x2, waiting for transfers between devices, over_dp(): return lax.ppermute(block, AXES, xor_route(count, partner_mask(rnd, width)))  77.8 us
    dot_general x3, matrix products, dot(): lax.dot_general(a, b, (dims, ((), ())), preferred_element_type=jnp.float32)  32.1 us
    pallas_call x1, Pallas kernels, final_call(): pl.pallas_call(body, grid=(rows // FINAL_ROWS,), in_specs=[block] * 3, ou...  6.22 us
    ppermute x2, starting transfers between devices, over_dp(): return lax.ppermute(block, AXES, xor_route(count, partner_mask(rnd, width)))  5.17 us
    unnamed x5, local copies, waits for them, and re-layouts  2.93 us
  transfers between devices with their start and end apart: 7, of which 2 were waited for; matrix products, arithmetic and copies ran while one was open for 9% of the time, Pallas kernels for 0%

profile of v1, /device:TPU:0, one launch (start us, length us, event | category | flops | bytes accessed | tf_op | source)
XLA Modules:
  0.0 134.7 jit_solution(15819249573363248942)
XLA Ops:
  0.6 2.1 %collective-permute-start.62 = (bf16[768,1152]{1,0:T(8,128)(2,1)}, bf16[768,1152]{1,0:T(8,128)(2,1)S(1)}, u32[]{:S(2)}, u32[]{:S(2)}) collective-permute-start(bf16[768,1152]{1,0:T(8,128)(2,1)} %param.68), channel_id=1, source_target_pairs={{0,2},{1,3},{2,0},{3,1},{4,6},{5,7},{6,4},{7,5},{8,10},{9,11},{10,... | collective-permute-start | bytes 5308424 | tf_op jit(solution)/shard_map/ppermute | solution.py:87
  3.4 41.4 %conditional.2 = (bf16[768,1152]{1,0:T(8,128)(2,1)}) conditional(s32[]{:T(128)} %bitcast.2, bf16[768,1152]{1,0:T(8,128)(2,1)} %param.69, bf16[768,1152]{1,0:T(8,128)(2,1)} %param.69, bf16[768,1152]{1,0:T(8,128)(2,1)} %param.69, bf16[768,1152]{1,0:T(8,128)(2,1)} %param.69, bf16[768,1152]{1,0:T(8,128)(2,1)} %param.69, ...), branch_computations={%region_0.0_spmd, %region_1.0_spmd, %region_2.0_spmd, %region_3.0_... | conditional | bytes 7077936 | solution.py:76
  3.4 2.6 %collective-permute-start.9 = (bf16[768,1152]{1,0:T(8,128)(2,1)}, bf16[768,1152]{1,0:T(8,128)(2,1)}, u32[]{:S(2)}, u32[]{:S(2)}) collective-permute-start(bf16[768,1152]{1,0:T(8,128)(2,1)} %param.9), channel_id=1, source_target_pairs={{0,40},{1,41},{2,42},{3,43},{4,44},{5,45},{6,46},{7,47},{8,32},{9,... | collective-permute-start | bytes 5308424 | tf_op jit(solution)/shard_map/cond/branch_9_fun/ppermute | solution.py:72
  6.0 38.8 %collective-permute-done.9 = bf16[768,1152]{1,0:T(8,128)(2,1)} collective-permute-done((bf16[768,1152]{1,0:T(8,128)(2,1)}, bf16[768,1152]{1,0:T(8,128)(2,1)}, u32[]{:S(2)}, u32[]{:S(2)}) %collective-permute-start.9) | collective-permute-done | bytes 1769504 | tf_op jit(solution)/shard_map/cond/branch_9_fun/ppermute | solution.py:72
  44.8 0.0 collective-permute-start.63
  46.1 0.9 fusion.7
  46.9 1.6 %constant_dynamic-update-slice_fusion.1 = bf16[1536,1152]{1,0:T(8,128)(2,1)S(1)} fusion(bf16[768,1152]{1,0:T(8,128)(2,1)} %param.68), kind=kLoop, calls=%fused_computation.15 | loop fusion | bytes 3538944
  48.6 0.3 constant_dynamic-update-slice_fusion
  48.9 17.7 %fusion.6 = (f32[1536]{0:T(1024)S(1)}, bf16[1536,1536]{0,1:T(8,128)(2,1)S(1)}) fusion(s32[1536]{0:T(1024)S(1)} %get-tuple-element.148, s32[1536]{0:T(1024)S(1)} %get-tuple-element.147, f32[]{:T(128)} %bitcast.11, bf16[1536,1152]{1,0:T(8,128)(2,1)S(1)} %constant_dynamic-update-slice_fusion, bf16[768,1152]{1,0:T(8,128)(2,1)S(1)} %collective-permute-done.63, ...), kind=kOutput, calls=%fused_computation.20 | convolution fusion | flops 5520751104 | bytes 11814920 | tf_op jit(solution)/shard_map/dot_general | solution.py:37
  66.6 6.3 %convolution_multiply_fusion = f32[1536,1152]{1,0:T(8,128)S(1)} fusion(bf16[1536,1536]{0,1:T(8,128)(2,1)S(1)} %get-tuple-element.142, bf16[1536,1152]{1,0:T(8,128)(2,1)S(1)} %constant_dynamic-update-slice_fusion, f32[]{:T(128)} %bitcast.10), kind=kOutput, calls=%fused_computation.2 | convolution fusion | flops 5437587456 | bytes 15335428 | tf_op jit(solution)/shard_map/dot_general | solution.py:37
  72.9 0.2 slice.22
  73.2 0.6 collective-permute-start.64
  73.7 0.3 collective-permute-start.65
  74.0 8.1 %convolution_multiply_fusion.1.image_part = f32[1536,1152]{1,0:T(8,128)S(1)} fusion(bf16[1536,1536]{0,1:T(8,128)(2,1)S(1)} %get-tuple-element.142, f32[]{:T(128)} %bitcast.8, bf16[768,1152]{1,0:T(8,128)(2,1)S(1)} %collective-permute-done.63, bf16[768,1152]{1,0:T(8,128)(2,1)} %get-tuple-element.149), kind=kOutput, calls=%fused_computation.3 | convolution fusion | flops 5444665344 | bytes 15335428 | tf_op jit(solution)/shard_map/dot_general | solution.py:37
  82.1 0.2 slice.33
  82.3 0.0 collective-permute-done.65
  82.3 1.8 %collective-permute-start.66 = (bf16[768,1152]{1,0:T(8,128)(2,1)S(1)}, bf16[768,1152]{1,0:T(8,128)(2,1)S(1)}, u32[]{:S(2)}, u32[]{:S(2)}) collective-permute-start(bf16[768,1152]{1,0:T(8,128)(2,1)S(1)} %slice.33), channel_id=1, source_target_pairs={{0,2},{1,3},{2,0},{3,1},{4,6},{5,7},{6,4},{7,5},{8,10},{9,11},{10,... | collective-permute-start | bytes 5308424 | tf_op jit(solution)/shard_map/ppermute | solution.py:105
  84.1 0.9 fusion.3
  85.0 0.5 fusion.2
  85.5 41.7 %conditional.3 = (bf16[768,1152]{1,0:T(8,128)(2,1)}) conditional(s32[]{:T(128)} %bitcast.2, bf16[768,1152]{1,0:T(8,128)(2,1)S(1)} %fusion.2, bf16[768,1152]{1,0:T(8,128)(2,1)S(1)} %fusion.2, bf16[768,1152]{1,0:T(8,128)(2,1)S(1)} %fusion.2, bf16[768,1152]{1,0:T(8,128)(2,1)S(1)} %fusion.2, ...), branch_computations={%region_31.32_spmd, %region_32.33_spmd, %region_33.34_spmd, %regio... | conditional | bytes 7077936 | solution.py:76
  85.5 2.6 %collective-permute-start.40 = (bf16[768,1152]{1,0:T(8,128)(2,1)S(1)}, bf16[768,1152]{1,0:T(8,128)(2,1)}, u32[]{:S(2)}, u32[]{:S(2)}) collective-permute-start(bf16[768,1152]{1,0:T(8,128)(2,1)S(1)} %param.40), channel_id=1, source_target_pairs={{0,40},{1,41},{2,42},{3,43},{4,44},{5,45},{6,46},{7,47},{8,32},{9,... | collective-permute-start | bytes 5308424 | tf_op jit(solution)/shard_map/cond/branch_9_fun/ppermute | solution.py:72
  88.1 39.1 %collective-permute-done.40 = bf16[768,1152]{1,0:T(8,128)(2,1)} collective-permute-done((bf16[768,1152]{1,0:T(8,128)(2,1)S(1)}, bf16[768,1152]{1,0:T(8,128)(2,1)}, u32[]{:S(2)}, u32[]{:S(2)}) %collective-permute-start.40) | collective-permute-done | bytes 1769504 | tf_op jit(solution)/shard_map/cond/branch_9_fun/ppermute | solution.py:72
  127.2 1.3 copy-done.1
  128.5 6.2 %shard_map.178 = (f32[768,1152]{1,0:T(8,128)}, f32[768,1152]{1,0:T(8,128)}) custom-call(f32[1536,1152]{1,0:T(8,128)} %copy-done, bf16[768,1152]{1,0:T(8,128)(2,1)} %copy-done.1, bf16[768,1152]{1,0:T(8,128)(2,1)} %get-tuple-element.150.text_grad), custom_call_target="tpu_custom_call" | custom-call | flops 884736 | bytes 14155776 | tf_op jit(solution)/shard_map/pallas_call | solution.py:48
  (9 shorter events, 0.0 us)
Async XLA Ops:
  0.6 47.9 %collective-permute-start.62 = (bf16[768,1152]{1,0:T(8,128)(2,1)}, bf16[768,1152]{1,0:T(8,128)(2,1)S(1)}, u32[]{:S(2)}, u32[]{:S(2)}) collective-permute-start(bf16[768,1152]{1,0:T(8,128)(2,1)} %param.68), channel_id=1, source_target_pairs={{0,2},{1,3},{2,0},{3,1},{4,6},{5,7},{6,4},{7,5},{8,10},{9,11},{10,... | collective-permute-start | bytes 5308424 | tf_op jit(solution)/shard_map/ppermute | solution.py:87
  3.4 41.4 %collective-permute-start.9 = (bf16[768,1152]{1,0:T(8,128)(2,1)}, bf16[768,1152]{1,0:T(8,128)(2,1)}, u32[]{:S(2)}, u32[]{:S(2)}) collective-permute-start(bf16[768,1152]{1,0:T(8,128)(2,1)} %param.9), channel_id=1, source_target_pairs={{0,40},{1,41},{2,42},{3,43},{4,44},{5,45},{6,46},{7,47},{8,32},{9,... | collective-permute-start | bytes 5308424 | tf_op jit(solution)/shard_map/cond/branch_9_fun/ppermute | solution.py:72
  44.8 4.1 %collective-permute-start.63 = (bf16[768,1152]{1,0:T(8,128)(2,1)}, bf16[768,1152]{1,0:T(8,128)(2,1)S(1)}, u32[]{:S(2)}, u32[]{:S(2)}) collective-permute-start(bf16[768,1152]{1,0:T(8,128)(2,1)} %get-tuple-element.149), channel_id=1, source_target_pairs={{0,1},{1,0},{2,3},{3,2},{4,5},{5,4},{6,7},{7,6},{8,9},{9,8},{10,11... | collective-permute-start | bytes 5308424 | tf_op jit(solution)/shard_map/ppermute | solution.py:89
  73.2 11.9 %collective-permute-start.64 = (f32[768,1152]{1,0:T(8,128)S(1)}, f32[768,1152]{1,0:T(8,128)S(1)}, u32[]{:S(2)}, u32[]{:S(2)}) collective-permute-start(f32[768,1152]{1,0:T(8,128)S(1)} %slice.22), channel_id=1, source_target_pairs={{0,1},{1,0},{2,3},{3,2},{4,5},{5,4},{6,7},{7,6},{8,9},{9,8},{10,11... | collective-permute-start | bytes 10616840 | tf_op jit(solution)/shard_map/ppermute | solution.py:98
  73.7 8.6 %collective-permute-start.65 = (f32[768]{0:T(1024)S(1)}, f32[768]{0:T(1024)S(1)}, u32[]{:S(2)}, u32[]{:S(2)}) collective-permute-start(f32[768]{0:T(1024)S(1)} %slice.24), channel_id=1, source_target_pairs={{0,2},{1,3},{2,0},{3,1},{4,6},{5,7},{6,4},{7,5},{8,10},{9,11},{10,... | collective-permute-start | bytes 9224 | tf_op jit(solution)/shard_map/ppermute | solution.py:103
  82.1 3.4 %copy-start = (f32[1536,1152]{1,0:T(8,128)}, f32[1536,1152]{1,0:T(8,128)S(1)}, u32[]{:S(2)}) copy-start(f32[1536,1152]{1,0:T(8,128)S(1)} %convolution_multiply_fusion.1.image_part) | copy-start | bytes 21233668
  82.3 44.9 %collective-permute-start.66 = (bf16[768,1152]{1,0:T(8,128)(2,1)S(1)}, bf16[768,1152]{1,0:T(8,128)(2,1)S(1)}, u32[]{:S(2)}, u32[]{:S(2)}) collective-permute-start(bf16[768,1152]{1,0:T(8,128)(2,1)S(1)} %slice.33), channel_id=1, source_target_pairs={{0,2},{1,3},{2,0},{3,1},{4,6},{5,7},{6,4},{7,5},{8,10},{9,11},{10,... | collective-permute-start | bytes 5308424 | tf_op jit(solution)/shard_map/ppermute | solution.py:105
  85.5 41.6 %collective-permute-start.40 = (bf16[768,1152]{1,0:T(8,128)(2,1)S(1)}, bf16[768,1152]{1,0:T(8,128)(2,1)}, u32[]{:S(2)}, u32[]{:S(2)}) collective-permute-start(bf16[768,1152]{1,0:T(8,128)(2,1)S(1)} %param.40), channel_id=1, source_target_pairs={{0,40},{1,41},{2,42},{3,43},{4,44},{5,45},{6,46},{7,47},{8,32},{9,... | collective-permute-start | bytes 5308424 | tf_op jit(solution)/shard_map/cond/branch_9_fun/ppermute | solution.py:72
  127.2 1.3 copy-start.1
